TPU v7x, 32 devices: a whole 2x2x4 slice. The times are simulated.
32 devices in a mesh: grp: 4 (over y, x), ta: 8 (over z, core).
Axes of the slice: x: 2, y: 2, z: 4, core: 2. Of those that a mesh axis runs over, the one named last changes fastest.
Arguments:
- transition: float32 [256, 256], replicated, may hold values from -1 to 1, as said below
- filtered_mean: float32 [512, 256], P(('grp', 'ta')), may hold values from -6 to 6
- filtered_cov: float32 [512, 256, 256], P(('grp', 'ta')), may hold values from -1 to 2, as said below
- pred_precision: float32 [512, 256, 256], P(('grp', 'ta')), may hold values from -1 to 2, as said below
Outputs:
- smoothed_mean: float32 [512, 256], P(('grp', 'ta'))
- smoothed_cov: float32 [512, 256, 256], P(('grp', 'ta'))
Inputs may be any that keep to these rules, and one draw needn't show every extreme that they name: transition is dominated by its diagonal. Each filtered_cov at a step is symmetric with a positive diagonal. Each pred_precision at a step is symmetric with a positive diagonal.
All inputs are finite; a program needn't handle non-finite values.
Results may differ from a plain program's by a relative error of at most 0.0003.
Values sent between devices are 32-bit elements; how exact they have to be, the bound alone decides.
A program may use at most 192 MiB of HBM per device.

v0:
```python
import jax
import jax.numpy as jnp
from jax import lax
from jax.sharding import PartitionSpec as P


def carried_in(value, axis, join, neutral):
    count, mine = (lax.axis_size(axis), lax.axis_index(axis))
    pieces = jax.tree.map(lambda part: lax.all_gather(part, axis), value)
    pieces = jax.tree.map(lambda part: part[::-1], pieces)
    mine = count - 1 - mine
    subtotal = jax.tree.map(
        lambda part, zero: jnp.full_like(part, 0) + jnp.asarray(zero, part.dtype), value, neutral
    )

    def step(position, subtotal):
        longer = join(subtotal, jax.tree.map(lambda part: part[position], pieces))
        return jax.tree.map(lambda new, old: jnp.where(position < mine, new, old), longer, subtotal)

    return lax.fori_loop(0, count - 1, step, subtotal)


def spread(value, axis, source):
    kept = jnp.where(lax.axis_index(axis) == source, value, 0).astype(value.dtype)
    return lax.psum(kept, axis)


def compose(earlier, later_part):
    highest = lax.Precision.HIGHEST
    first_e, first_g, first_l = earlier
    second_e, second_g, second_l = later_part
    joined_e = jnp.matmul(first_e, second_e, precision=highest)
    joined_g = jnp.einsum("...ij,...j->...i", first_e, second_g, precision=highest) + first_g
    inner = jnp.matmul(first_e, second_l, precision=highest)
    joined_l = jnp.matmul(inner, jnp.swapaxes(first_e, -1, -2), precision=highest) + first_l
    return (joined_e, joined_g, joined_l)


def reverse_order(higher, lower):
    return compose(lower, higher)


def body(transition, filtered_mean, filtered_cov, pred_precision):
    highest = lax.Precision.HIGHEST
    steps_here = filtered_cov.shape[0]
    state_width = transition.shape[0]
    moved_cov = jnp.einsum("ij,tjk->tik", transition, filtered_cov, precision=highest)
    gain_mats = jnp.einsum("tji,tjl->til", moved_cov, pred_precision, precision=highest)
    at_end = jnp.logical_and(
        lax.axis_index("grp") == lax.axis_size("grp") - 1,
        lax.axis_index("ta") == lax.axis_size("ta") - 1,
    )
    positions = jnp.arange(steps_here, dtype=jnp.int32)
    keep_mask = jnp.where(jnp.logical_and(at_end, positions == steps_here - 1), 0.0, 1.0).astype(
        jnp.float32
    )
    gain_mats = gain_mats * keep_mask[:, None, None]
    predicted = jnp.einsum("ij,tj->ti", transition, filtered_mean, precision=highest)
    offsets = filtered_mean - jnp.einsum("tij,tj->ti", gain_mats, predicted, precision=highest)
    leftovers = filtered_cov - jnp.einsum("tij,tjk->tik", gain_mats, moved_cov, precision=highest)

    def absorb(accum, entries):
        return (compose(entries, accum), None)

    start_elem = (gain_mats[-1], offsets[-1], leftovers[-1])
    total_local, unused = lax.scan(
        absorb, start_elem, (gain_mats[:-1], offsets[:-1], leftovers[:-1]), reverse=True
    )
    identity = (
        jnp.eye(state_width, dtype=jnp.float32),
        jnp.zeros((state_width,), jnp.float32),
        jnp.zeros((state_width, state_width), jnp.float32),
    )
    after_group = carried_in(total_local, "ta", reverse_order, identity)
    group_part = compose(total_local, after_group)
    group_whole = (
        spread(group_part[0], "ta", 0),
        spread(group_part[1], "ta", 0),
        spread(group_part[2], "ta", 0),
    )
    after_groups = carried_in(group_whole, "grp", reverse_order, identity)
    carried = compose(after_group, after_groups)

    def sweep(state_pair, entries):
        mean_next, cov_next = state_pair
        gain_mat, offset, leftover = entries
        mean_out = jnp.dot(gain_mat, mean_next, precision=highest) + offset
        inner = jnp.dot(gain_mat, cov_next, precision=highest)
        cov_out = jnp.dot(inner, gain_mat.T, precision=highest) + leftover
        return ((mean_out, cov_out), (mean_out, cov_out))

    final_state, outputs = lax.scan(
        sweep, (carried[1], carried[2]), (gain_mats, offsets, leftovers), reverse=True
    )
    return (outputs[0], outputs[1])


def solution(mesh):
    return jax.shard_map(
        body,
        mesh=mesh,
        in_specs=(
            P(),
            P(("grp", "ta"), None),
            P(("grp", "ta"), None, None),
            P(("grp", "ta"), None, None),
        ),
        out_specs=(P(("grp", "ta"), None), P(("grp", "ta"), None, None)),
        check_vma=False,
    )
```

profile of v0, /device:TPU:0, one launch (start us, length us, event | category | flops | bytes accessed | tf_op | source)
XLA Modules:
  0.0 411.0 jit_solution(9666156387690830090)
XLA Ops:
  8.1 8.8 %fusion.64 = f32[16,256,256]{2,1,0:T(8,128)S(1)} fusion(f32[16,256,256]{2,1,0:T(8,128)} %param.14, f32[256,256]{1,0:T(8,128)S(1)} %copy-done), kind=kOutput, calls=%fused_computation.86 | convolution fusion | flops 3221225472 | bytes 8650752 | tf_op jit(solution)/shard_map/ij,tjk->tik/dot_general | solution.py:47
  17.0 4.5 %convolution_multiply_fusion = f32[16,256,256]{2,1,0:T(8,128)S(1)} fusion(f32[16,256,256]{2,1,0:T(8,128)S(1)} %fusion.64, f32[16,256,256]{2,1,0:T(8,128)S(1)} %copy-done.7, f32[16]{0:T(128)S(1)} %and_select_fusion), kind=kOutput, calls=%fused_computation.76 | convolution fusion | flops 3222274048 | bytes 12582976 | tf_op jit(solution)/shard_map/tji,tjl->til/dot_general | solution.py:48
  21.5 4.4 %convolution_subtract_fusion = f32[16,256,256]{2,1,0:T(8,128)S(1)} fusion(f32[16,256,256]{2,1,0:T(8,128)S(1)} %copy-done.5, f32[16,256,256]{2,1,0:T(8,128)S(1)} %convolution_multiply_fusion, f32[16,256,256]{2,1,0:T(8,128)S(1)} %fusion.64), kind=kOutput, calls=%fused_computation.75 | convolution fusion | flops 3222274048 | bytes 16777216 | tf_op jit(solution)/shard_map/tij,tjk->tik/dot_general | solution.py:60
  26.0 2.5 slice.29
  29.2 2.3 slice.27
  31.8 3.8 fusion.67
  35.6 82.2 %while.72 = (s32[]{:T(128)}, f32[256,256]{1,0:T(8,128)S(1)}, f32[256]{0:T(256)S(1)}, f32[256,256]{1,0:T(8,128)S(1)}, f32[15,256,256]{2,1,0:T(8,128)}, /*index=5*...) while((s32[]{:T(128)}, f32[256,256]{1,0:T(8,128)S(1)}, f32[256]{0:T(256)S(1)}, ...), condition=%wide.region_1.2_spmd, body=%wide.region_0.1_spmd.sunk | while | flops 604832000 | bytes 3416185 | solution.py:66
  37.0 1.4 convolution_add_fusion.7
  42.5 1.4 convolution_add_fusion.7
  47.9 1.4 convolution_add_fusion.7
  53.4 1.4 convolution_add_fusion.7
  58.9 1.4 convolution_add_fusion.7
  64.4 1.4 convolution_add_fusion.7
  69.9 1.4 convolution_add_fusion.7
  75.3 1.4 convolution_add_fusion.7
  80.8 1.4 convolution_add_fusion.7
  86.3 1.4 convolution_add_fusion.7
  91.8 1.4 convolution_add_fusion.7
  97.3 1.4 convolution_add_fusion.7
  102.8 1.4 convolution_add_fusion.7
  108.2 1.4 convolution_add_fusion.7
  113.7 1.4 convolution_add_fusion.7
  119.4 13.4 %all-gather.3 = f32[8,1,256]{2,1,0:T(1,128)S(1)} all-gather(f32[1,1,256]{2,1,0:T(1,128)S(1)} %bitcast.227), channel_id=3, replica_groups=mesh['grp'=4,'ta'=8] {'ta'}, dimensions={0}, use_global_device_ids=true | all-gather | bytes 9216 | tf_op jit(solution)/shard_map/all_gather | solution.py:9
  132.9 17.7 %all-gather.14.cloned.1.call-done = f32[2048,256]{1,0:T(8,128)} async-done(((f32[256,256]{1,0:T(8,128)}), f32[2048,256]{1,0:T(8,128)}) %all-gather.14.cloned.1.call-update) | async-done | bytes 2097168 | tf_op jit(solution)/shard_map/all_gather | solution.py:9
  150.5 1.8 rev.18
  152.4 28.4 %all-gather.16.cloned.1.call-done = f32[2048,256]{1,0:T(8,128)} async-done(((f32[256,256]{1,0:T(8,128)}), f32[2048,256]{1,0:T(8,128)}) %all-gather.16.cloned.1.call-update) | async-done | bytes 2097168 | tf_op jit(solution)/shard_map/all_gather | solution.py:9
  180.8 3.0 rev.20
  183.8 18.3 %while.74 = (s32[]{:T(128)}, f32[256,256]{1,0:T(8,128)S(1)}, f32[256]{0:T(256)S(1)}, f32[256,256]{1,0:T(8,128)S(1)}, s32[]{:T(128)}, /*index=5*/f32[8,256,256]{2...) while((s32[]{:T(128)}, f32[256,256]{1,0:T(8,128)S(1)}, ...), condition=%wide.region_3.4_spmd.clone, body=%wide.region_2.3_spmd.clone.sunk | while | flops 605094912 | bytes 3943566 | solution.py:20
  184.2 1.4 fusion.173
  186.8 1.4 fusion.173
  189.5 1.4 fusion.173
  192.1 1.4 fusion.173
  194.7 1.4 fusion.173
  197.3 1.4 fusion.173
  199.9 1.4 fusion.173
  202.5 2.1 fusion.62
  205.8 55.9 %all-reduce.3.cloned.1.call-done = (f32[1,256,256]{2,1,0:T(8,128)}, f32[1,256,256]{2,1,0:T(8,128)}) async-done(((f32[1,256,256]{2,1,0:T(8,128)}, f32[1,256,256]{2,1,0:T(8,128)}), (f32[1,256,256]{2,1,0:T(8,128)}, f32[1,256,256]{2,1,0:T(8,128)})) %all-reduce.3.cloned.1.call-update) | async-done | bytes 524304 | tf_op jit(solution)/shard_map/psum | solution.py:25
  262.7 13.6 %psum.22 = f32[1,256]{1,0:T(1,128)S(1)} all-reduce(f32[1,256]{1,0:T(1,128)S(1)} %bitcast.234), channel_id=1, replica_groups=mesh['grp'=4,'ta'=8] {'ta'}, use_global_device_ids=true, to_apply=%region_5.6 | all-reduce | flops 256 | bytes 2048 | tf_op jit(solution)/shard_map/psum | solution.py:25
  276.3 8.0 %all-gather.4 = f32[4,1,256]{2,1,0:T(1,128)S(1)} all-gather(f32[1,1,256]{2,1,0:T(1,128)S(1)} %bitcast.235), channel_id=1, replica_groups=mesh['grp'=4,'ta'=8] {'grp'}, dimensions={0}, use_global_device_ids=true | all-gather | bytes 5120 | tf_op jit(solution)/shard_map/all_gather | solution.py:9
  284.3 4.9 %all-gather.10.cloned.1.call-done = f32[4,256,256]{2,1,0:T(8,128)} async-done(((f32[1,256,256]{2,1,0:T(8,128)}), f32[4,256,256]{2,1,0:T(8,128)}) %all-gather.10.cloned.1.call-update) | async-done | bytes 1048592 | tf_op jit(solution)/shard_map/all_gather | solution.py:9
  290.5 27.2 %all-gather.12.cloned.1.call-done = f32[4,256,256]{2,1,0:T(8,128)} async-done(((f32[1,256,256]{2,1,0:T(8,128)}), f32[4,256,256]{2,1,0:T(8,128)}) %all-gather.12.cloned.1.call-update) | async-done | bytes 1048592 | tf_op jit(solution)/shard_map/all_gather | solution.py:9
  319.0 3.8 while.75
  323.9 2.5 broadcast_in_dim.51
  326.4 77.5 %while.73 = (s32[]{:T(128)}, f32[256]{0:T(256)S(1)}, f32[256,256]{1,0:T(8,128)S(1)}, f32[16,256]{1,0:T(8,128)S(1)}, f32[16,256,256]{2,1,0:T(8,128)}, /*index=5*/...) while((s32[]{:T(128)}, f32[256]{0:T(256)S(1)}, ...), condition=%wide.region_10.11_spmd, body=%wide.region_9.10_spmd.sunk | while | flops 403505408 | bytes 2369673 | solution.py:92
  329.1 2.2 bitcast_dynamic-update-slice_fusion.2
  333.9 2.2 bitcast_dynamic-update-slice_fusion.2
  338.8 2.2 bitcast_dynamic-update-slice_fusion.2
  343.6 2.2 bitcast_dynamic-update-slice_fusion.2
  347.1 1.3 fusion.162
  348.5 2.2 bitcast_dynamic-update-slice_fusion.2
  353.3 2.2 bitcast_dynamic-update-slice_fusion.2
  356.8 1.3 fusion.162
  358.1 2.2 bitcast_dynamic-update-slice_fusion.2
  363.0 2.2 bitcast_dynamic-update-slice_fusion.2
  366.5 1.3 fusion.162
  367.8 2.2 bitcast_dynamic-update-slice_fusion.2
  372.7 2.2 bitcast_dynamic-update-slice_fusion.2
  376.2 1.3 fusion.162
  377.5 2.2 bitcast_dynamic-update-slice_fusion.2
  382.4 2.2 bitcast_dynamic-update-slice_fusion.2
  387.2 2.2 bitcast_dynamic-update-slice_fusion.2
  392.0 2.2 bitcast_dynamic-update-slice_fusion.2
  396.9 2.2 bitcast_dynamic-update-slice_fusion.2
  401.7 2.2 bitcast_dynamic-update-slice_fusion.2
  (288 shorter events, 118.6 us)
Async XLA Ops:
  7.2 1.0 copy-start
  7.2 143.4 %all-gather.14.cloned.1.call-start = ((), (), s32[]{:S(2)}) async-start(), calls=%async_computation.2 | async-start | bytes 2359296 | tf_op jit(solution)/shard_map/all_gather | solution.py:9
  8.1 8.8 %copy-start.7 = (f32[16,256,256]{2,1,0:T(8,128)S(1)}, f32[16,256,256]{2,1,0:T(8,128)}, u32[]{:S(2)}) copy-start(f32[16,256,256]{2,1,0:T(8,128)} %param.15) | copy-start | bytes 12582916
  17.0 4.5 %copy-start.5 = (f32[16,256,256]{2,1,0:T(8,128)S(1)}, f32[16,256,256]{2,1,0:T(8,128)}, u32[]{:S(2)}) copy-start(f32[16,256,256]{2,1,0:T(8,128)} %param.14) | copy-start | bytes 12582916
  21.5 10.2 %copy-start.1 = (f32[16,256,256]{2,1,0:T(8,128)}, f32[16,256,256]{2,1,0:T(8,128)S(1)}, u32[]{:S(2)}) copy-start(f32[16,256,256]{2,1,0:T(8,128)S(1)} %convolution_multiply_fusion) | copy-start | bytes 12582916
  26.0 3.2 copy-start.4
  29.2 2.3 copy-start.8
  117.9 0.7 copy-start.2
  117.9 0.8 copy-start.6
  118.6 62.2 %all-gather.16.cloned.1.call-start = ((), (), s32[]{:S(2)}) async-start(), calls=%async_computation.3 | async-start | bytes 2359296 | tf_op jit(solution)/shard_map/all_gather | solution.py:9
  119.3 142.3 %all-reduce.3.cloned.1.call-start = ((), (), s32[]{:S(2)}) async-start(), calls=%async_computation.4 | async-start | bytes 1048576 | tf_op jit(solution)/shard_map/psum | solution.py:25
  183.8 18.3 %copy-start.3 = (f32[256,256]{1,0:T(8,128)S(1)}, f32[256,256]{1,0:T(8,128)}, u32[]{:S(2)}) copy-start(f32[256,256]{1,0:T(8,128)} %copy-done.2) | copy-start | bytes 786436
  205.7 83.5 %all-gather.10.cloned.1.call-start = ((), (), s32[]{:S(2)}) async-start(), calls=%async_computation | async-start | bytes 1310720 | tf_op jit(solution)/shard_map/all_gather | solution.py:9
  261.7 56.0 %all-gather.12.cloned.1.call-start = ((), (), s32[]{:S(2)}) async-start(), calls=%async_computation.1 | async-start | bytes 1310720 | tf_op jit(solution)/shard_map/all_gather | solution.py:9
  403.9 0.6 copy-start.9
Sparse Core Ops, SparseCore 0:
  118.7 31.7 all-gather.13
  152.1 28.5 all-gather.15
  205.8 55.8 all-reduce.2
  263.5 25.6 all-gather.9
  291.1 26.5 all-gather.11
where the time goes:
time: 415 us; the launch traced here: 411 us
  matrix products  203 us (49%)
  waiting for transfers between devices  135 us (33%)
  blocking collectives  35 us (8%)
  local copies, waits for them, and re-layouts  21.4 us (5%)
  between operations  14.1 us (3%)
    all_gather x4, waiting for transfers between devices, carried_in(): pieces = jax.tree.map(lambda part: lax.all_gather(part, axis), value)  78.2 us
    psum x1, waiting for transfers between devices, spread(): return lax.psum(kept, axis)  55.9 us
    dot_general x27, matrix products, compose(): jnp.matmul(inner, jnp.swapaxes(first_e, -1, -2), precision=highest)  35.3 us
    dot_general x16, matrix products, sweep(): cov_out = jnp.dot(inner, gain_mat.T, precision=highest) + leftover  34.5 us
    dot_general x27, matrix products, compose(): inner = jnp.matmul(first_e, second_l, precision=highest)  24.6 us
    dot_general x23, matrix products, compose(): joined_e = jnp.matmul(first_e, second_e, precision=highest)  23.8 us
    dot_general x27, matrix products, compose(): jnp.einsum('...ij,...j->...i', first_e, second_g, precision=highest)  21.7 us
    all_gather x2, blocking collectives, carried_in(): pieces = jax.tree.map(lambda part: lax.all_gather(part, axis), value)  21.4 us
  transfers between devices with their start and end apart: 5, of which 5 were waited for; matrix products, arithmetic and copies ran while one was open for 1% of the time, Pallas kernels for 0%

commit v1 on v0

v1 whole, which is shorter than its diff:
```python
import functools
import jax
import jax.numpy as jnp
from jax import lax
from jax.experimental import pallas as pl
from jax.experimental.pallas import tpu as pltpu
from jax.sharding import PartitionSpec as P

F32 = jnp.float32
BF16 = jnp.bfloat16
MESH = pl.DeviceIdType.MESH
PAD = 16


def split(x):
    hi = x.astype(BF16)
    lo = (x - hi.astype(F32)).astype(BF16)
    return hi, lo


def left(x):
    hi, lo = split(x)
    return jnp.concatenate([hi, hi, lo], axis=1)


def right(x):
    hi, lo = split(x)
    return jnp.concatenate([hi, lo, hi], axis=0)


def right_t(x):
    hi, lo = split(x)
    return jnp.concatenate([hi, lo, hi], axis=1)


def split3(x):
    hi = x.astype(BF16)
    rest = x - hi.astype(F32)
    mid = rest.astype(BF16)
    return hi, mid, (rest - mid.astype(F32)).astype(BF16)


def left6(x):
    hi, mid, lo = split3(x)
    return jnp.concatenate([hi, hi, mid, hi, mid, lo], axis=1)


def right6(x, axis):
    hi, mid, lo = split3(x)
    return jnp.concatenate([hi, mid, hi, lo, mid, hi], axis=axis)


def left4(x):
    hi, lo = split(x)
    return jnp.concatenate([hi, hi, lo, lo], axis=1)


def right4(x, axis):
    hi, lo = split(x)
    return jnp.concatenate([hi, lo, hi, lo], axis=axis)


def mm(a3, b3):
    return lax.dot_general(a3, b3, (((1,), (0,)), ((), ())), preferred_element_type=F32)


def mm_t(a3, b3):
    return lax.dot_general(a3, b3, (((1,), (1,)), ((), ())), preferred_element_type=F32)


def wide(row):
    return jnp.broadcast_to(row[:1, :], (PAD, row.shape[1]))


def push(inner, row, e_t, cut=left):
    n = inner.shape[0]
    out = mm_t(cut(jnp.concatenate([inner, wide(row)], axis=0)), e_t)
    return out[:n], out[n:n + 1]


def compose(first, second, want_e=True):
    e1, g1, l1 = first
    e2, g2, l2 = second
    e1l = left(e1)
    inner = mm(e1l, right(l2))
    e = mm(e1l, right(e2)) if want_e else None
    l, g = push(inner, g2, right_t(e1))
    return e, g + g1, l + l1


def local_kernel(blocks, length, a_ref, m_ref, p_ref, q_ref, e_ref, l_ref, g_ref, tot_ref, acc_e, acc_l, acc_g):
    s = pl.program_id(0)
    n = a_ref.shape[0]
    last_dev = jnp.logical_and(
        lax.axis_index("grp") == lax.axis_size("grp") - 1,
        lax.axis_index("ta") == lax.axis_size("ta") - 1,
    )
    at = right6(a_ref[...], 1)
    rows = [p_ref[b, 0] for b in range(blocks)] + [wide(m_ref[b, 0]) for b in range(blocks)]
    moved = mm_t(left6(jnp.concatenate(rows, axis=0)), at)
    gains = []
    for b in range(blocks):
        gain = mm(left6(moved[b * n:(b + 1) * n]), right6(q_ref[b, 0], 0))
        if b == blocks - 1:
            gain = jnp.where(jnp.logical_and(last_dev, s == 0), jnp.zeros_like(gain), gain)
        gains.append(gain)

    def finish(b, e, inner, row):
        start = blocks * n + b * PAD
        l, g = push(inner - moved[b * n:(b + 1) * n], row - moved[start:start + 1], right4(gains[b], 1), left4)
        l = l + p_ref[b, 0]
        g = g + m_ref[b, 0]
        e_ref[b, 0] = e
        l_ref[b, 0] = l
        g_ref[b, 0] = g
        acc_e[b] = e
        acc_l[b] = l
        acc_g[b] = jnp.broadcast_to(g, (8, n))

    @pl.when(s == 0)
    def _():
        for b in range(blocks):
            finish(b, gains[b], jnp.zeros((n, n), F32), jnp.zeros((1, n), F32))

    @pl.when(s > 0)
    def _():
        for b in range(blocks):
            gl = left4(gains[b])
            e = mm(gl, right4(acc_e[b], 0))
            inner = mm(gl, right4(acc_l[b], 0))
            finish(b, e, inner, acc_g[b][:1])

    @pl.when(s == length - 1)
    def _():
        parts = [(acc_e[b], acc_g[b][:1], acc_l[b]) for b in range(blocks)]
        while len(parts) > 1:
            parts = [compose(parts[i], parts[i + 1]) for i in range(0, len(parts), 2)]
        e, g, l = parts[0]
        half = n + PAD
        tot_ref[0:n] = l
        tot_ref[n:half] = wide(g)
        tot_ref[half:half + n] = e
        tot_ref[half + n:2 * half] = jnp.zeros((PAD, n), F32)


def exchange_kernel(sizes, t_ref, o_ref, tot, exc, got, s_sem, r_sem, s2_sem, r2_sem):
    n = t_ref.shape[1]
    half = n + PAD
    grp, ta = lax.axis_index("grp"), lax.axis_index("ta")
    core = lax.rem(ta, 2)
    sib = (grp, ta + 1 - 2 * core)
    partners = []
    for name, size in sizes:
        step = 1
        while step < size:
            pos = ta if name == "ta" else grp
            bit = lax.rem(lax.div(pos, step), 2)
            other = pos + step - 2 * step * bit
            partners.append(((grp, other) if name == "ta" else (other, ta), bit))
            step *= 2
    rounds = len(partners)
    barrier = pltpu.get_barrier_semaphore()
    for dev, _ in partners:
        pl.semaphore_signal(barrier, inc=1, device_id=dev, device_id_type=MESH)
    pl.semaphore_wait(barrier, rounds)

    def copy(src, dst, a, b, dev):
        return pltpu.make_async_remote_copy(
            src_ref=src, dst_ref=dst, send_sem=a, recv_sem=b, device_id=dev, device_id_type=MESH)

    def read(ref):
        return ref[half:half + n], ref[n:n + 8][:1], ref[0:n]

    def write(ref, val):
        e, g, l = val
        ref[0:n] = l
        ref[n:half] = wide(g)
        ref[half:half + n] = e
        ref[half + n:2 * half] = jnp.zeros((PAD, n), F32)

    def pick(c, x, y):
        return tuple(jnp.where(c, i, j) for i, j in zip(x, y))

    for k, (dev, bit) in enumerate(partners):
        final = k == rounds - 1
        low = bit == 0
        src = t_ref if k == 0 else tot.at[k]
        if k == 0:
            send = copy(src, got.at[k], s_sem.at[k], r_sem.at[k], dev)
            send.start()
        else:
            size = half // 2 if final else half
            rows = pl.ds(pl.multiple_of(core * size, 8), size)
            send = copy(src.at[rows], got.at[k, rows], s_sem.at[k], r_sem.at[k], dev)
            send.start()
        if k > 1:
            old, new = exc.at[(k - 1) % 2], got.at[k - 1]
            was_low = partners[k - 1][1] == 0
            mine = read(old)
            write(exc.at[k % 2], pick(was_low, compose(mine, read(new)), mine))
        elif k == 1:
            was_low = partners[0][1] == 0
            eye = (lax.broadcasted_iota(jnp.int32, (n, n), 0) == lax.broadcasted_iota(jnp.int32, (n, n), 1)).astype(F32)
            write(exc.at[1], pick(was_low, read(got.at[0]), (eye, jnp.zeros((1, n), F32), jnp.zeros((n, n), F32))))
        send.wait()
        if k > 0:
            swap = copy(got.at[k, rows], got.at[k, rows], s2_sem.at[k], r2_sem.at[k], sib)
            swap.start()
            swap.wait()
        if not final:
            mine, theirs = read(src), read(got.at[k])
            write(tot.at[k + 1], compose(pick(low, mine, theirs), pick(low, theirs, mine)))
    mine = read(exc.at[(rounds - 1) % 2])
    ref = got.at[rounds - 1]
    later = (None, ref[n:n + 8][:1], ref[0:n])
    _, g, l = compose(mine, later, want_e=False)
    o_ref[0:n] = jnp.where(low, l, mine[2])
    o_ref[n:half] = wide(jnp.where(low, g, mine[1]))


def apply_kernel(length, c_ref, e_ref, l_ref, g_ref, m_ref, o_ref, carry):
    n = e_ref.shape[-1]

    @pl.when(pl.program_id(0) == 0)
    def _():
        carry[...] = c_ref[...]

    cov, mean = right(carry[0:n]), carry[n:n + 8][:1]
    for i in reversed(range(length)):
        e = e_ref[0, i]
        l, g = push(mm(left(e), cov), mean, right_t(e))
        l = l + l_ref[0, i]
        g = g + g_ref[0, i]
        o_ref[0, i] = l
        m_ref[0, i] = g
    carry[0:n] = l
    carry[n:n + PAD] = wide(g)


def body(transition, filtered_mean, filtered_cov, pred_precision):
    steps, n = filtered_mean.shape
    blocks = 4
    length = steps // blocks
    half = n + PAD
    mat = (blocks, length, n, n)
    vec = (blocks, length, 1, n)
    limit = 56 * 1024 * 1024
    flops = 2 * n * n * n * 3
    by_pos = lambda shape: pl.BlockSpec((blocks, 1) + shape, lambda s: (0, length - 1 - s, 0, 0))
    whole = lambda shape: pl.BlockSpec(shape, lambda s: (0,) * len(shape))
    e, l, g, total = pl.pallas_call(
        functools.partial(local_kernel, blocks, length),
        grid=(length,),
        in_specs=[whole((n, n)), by_pos((1, n)), by_pos((n, n)), by_pos((n, n))],
        out_specs=[by_pos((n, n)), by_pos((n, n)), by_pos((1, n)), whole((2 * half, n))],
        out_shape=[
            jax.ShapeDtypeStruct(mat, F32),
            jax.ShapeDtypeStruct(mat, F32),
            jax.ShapeDtypeStruct(vec, F32),
            jax.ShapeDtypeStruct((2 * half, n), F32),
        ],
        scratch_shapes=[
            pltpu.VMEM((blocks, n, n), F32),
            pltpu.VMEM((blocks, n, n), F32),
            pltpu.VMEM((blocks, 8, n), F32),
        ],
        compiler_params=pltpu.CompilerParams(vmem_limit_bytes=limit),
        cost_estimate=pl.CostEstimate(flops=80 * flops, bytes_accessed=16 * steps * n * n, transcendentals=0),
    )(transition, filtered_mean.reshape(vec), filtered_cov.reshape(mat), pred_precision.reshape(mat))

    sizes = (("ta", lax.axis_size("ta")), ("grp", lax.axis_size("grp")))
    rounds = sum(size.bit_length() - 1 for _, size in sizes)
    vmem = pl.BlockSpec(memory_space=pltpu.VMEM)
    carried = pl.pallas_call(
        functools.partial(exchange_kernel, sizes),
        in_specs=[vmem],
        out_specs=vmem,
        out_shape=jax.ShapeDtypeStruct((half, n), F32),
        scratch_shapes=[
            pltpu.VMEM((rounds, 2 * half, n), F32),
            pltpu.VMEM((2, 2 * half, n), F32),
            pltpu.VMEM((rounds, 2 * half, n), F32),
        ] + [pltpu.SemaphoreType.DMA((rounds,))] * 4,
        compiler_params=pltpu.CompilerParams(
            vmem_limit_bytes=limit, collective_id=0, has_side_effects=True),
    )(total)

    back = lambda shape: pl.BlockSpec((1, length) + shape, lambda s: (blocks - 1 - s, 0, 0, 0))
    mean, cov = pl.pallas_call(
        functools.partial(apply_kernel, length),
        grid=(blocks,),
        in_specs=[whole((half, n)), back((n, n)), back((n, n)), back((1, n))],
        out_specs=[back((1, n)), back((n, n))],
        out_shape=[jax.ShapeDtypeStruct(vec, F32), jax.ShapeDtypeStruct(mat, F32)],
        scratch_shapes=[pltpu.VMEM((half, n), F32)],
        compiler_params=pltpu.CompilerParams(vmem_limit_bytes=limit),
    )(carried, e, l, g)
    return mean.reshape(steps, n), cov.reshape(steps, n, n)


def solution(mesh):
    return jax.shard_map(
        body,
        mesh=mesh,
        in_specs=(
            P(),
            P(("grp", "ta"), None),
            P(("grp", "ta"), None, None),
            P(("grp", "ta"), None, None),
        ),
        out_specs=(P(("grp", "ta"), None), P(("grp", "ta"), None, None)),
        check_vma=False,
    )
```

time: 415 us -> 91.3 us (0.22)
  matrix products: 203 us -> 0 us
  waiting for transfers between devices: 135 us -> 0 us
  Pallas kernels: 0 us -> 87.6 us
  blocking collectives: 35 us -> 0 us
  local copies, waits for them, and re-layouts: 21.4 us -> 1.96 us
  between operations: 14.1 us -> 0.64 us
    dot_general x157 -> x0, matrix products: 203 us -> none  [the longest x27 35.3 us: compose(): jnp.matmul(inner, jnp.swapaxes(first_e, -1, -2), precision=highest)]
    pallas_call x0 -> x3, Pallas kernels: none -> 87.6 us  [the longest x1 52.2 us: body(): pl.pallas_call(functools.partial(exchange_kernel, sizes), in_specs=[vmem]...]
    all_gather x4 -> x0, waiting for transfers between devices: 78.2 us -> none  [carried_in(): pieces = jax.tree.map(lambda part: lax.all_gather(part, axis), value)]
    psum x1 -> x0, waiting for transfers between devices: 55.9 us -> none  [spread(): return lax.psum(kept, axis)]
    all_gather x2 -> x0, blocking collectives: 21.4 us -> none  [carried_in(): pieces = jax.tree.map(lambda part: lax.all_gather(part, axis), value)]
    psum x1 -> x0, blocking collectives: 13.6 us -> none  [spread(): return lax.psum(kept, axis)]
    rev x6 -> x0, local copies, waits for them, and re-layouts: 7.51 us -> none  [carried_in(): pieces = jax.tree.map(lambda part: part[::-1], pieces)]
    slice x3 -> x0, local copies, waits for them, and re-layouts: 4.79 us -> none  [the longest x1 2.5 us: body(): leftovers[:-1]]
  transfers between devices with their start and end apart: 5 -> 0, of which waited for: 5 -> 0; matrix products, arithmetic and copies ran while one was open for 1% -> 0% of each run, Pallas kernels for 0% -> 0%
where the time goes in v1:
time: 91.3 us; the launch traced here: 91 us
  Pallas kernels  87.6 us (96%)
  local copies, waits for them, and re-layouts  1.96 us (2%)
    pallas_call x1, Pallas kernels, body(): pl.pallas_call(functools.partial(exchange_kernel, sizes), in_specs=[vmem]...  52.2 us
    pallas_call x1, Pallas kernels, body(): pl.pallas_call(functools.partial(local_kernel, blocks, length), grid=(len...  26.7 us
    pallas_call x1, Pallas kernels, body(): pl.pallas_call(functools.partial(apply_kernel, length), grid=(blocks,), i...  8.75 us

profile of v1, /device:TPU:0, one launch (start us, length us, event | category | flops | bytes accessed | tf_op | source)
XLA Modules:
  0.0 91.0 jit_solution(6199951746902870972)
XLA Ops:
  0.6 1.3 %reshape.19.m_ref = f32[4,4,1,256]{3,2,1,0:T(1,128)} reshape(f32[16,256]{1,0:T(8,128)} %param.5) | data formatting | bytes 32768 | tf_op jit(solution)/shard_map/reshape | solution.py:269
  2.0 26.7 %shard_map.59 = (f32[4,4,256,256]{3,2,1,0:T(8,128)}, f32[4,4,256,256]{3,2,1,0:T(8,128)}, f32[4,4,1,256]{3,2,1,0:T(1,128)}, f32[544,256]{1,0:T(8,128)}) custom-call(f32[256,256]{1,0:T(8,128)} %a_ref.1, f32[4,4,1,256]{3,2,1,0:T(1,128)} %reshape.19.m_ref, f32[4,4,256,256]{3,2,1,0:T(8,128)} %bitcast.3, f32[4,4,256,256]{3,2,1,0:T(8,128)} %bitcast.4), custom_call_target="tpu_custom_call" | custom-call | flops 8053063680 | bytes 16777216 | tf_op jit(solution)/shard_map/pallas_call | solution.py:251
  28.7 52.2 %shard_map.60.c_ref = f32[272,256]{1,0:T(8,128)} custom-call(f32[544,256]{1,0:T(8,128)} %get-tuple-element.8.t_ref), custom_call_target="tpu_custom_call" | custom-call | tf_op jit(solution)/shard_map/pallas_call | solution.py:274
  80.9 8.8 %shard_map.61 = (f32[4,4,1,256]{3,2,1,0:T(1,128)}, f32[4,4,256,256]{3,2,1,0:T(8,128)}) custom-call(f32[272,256]{1,0:T(8,128)} %shard_map.60.c_ref, f32[4,4,256,256]{3,2,1,0:T(8,128)} %get-tuple-element.9.e_ref, f32[4,4,256,256]{3,2,1,0:T(8,128)} %get-tuple-element.10.l_ref, f32[4,4,1,256]{3,2,1,0:T(1,128)} %get-tuple-element.11.g_ref), custom_call_target="tpu_custom_call" | custom-call | tf_op jit(solution)/shard_map/pallas_call | solution.py:289
  89.6 0.8 reduce
  90.4 0.6 reshape.22

commit v2 on v1

--- a/solution.py
+++ b/solution.py
@@ -40,14 +40,14 @@
     return hi, mid, (rest - mid.astype(F32)).astype(BF16)
 
 
-def left6(x):
+def left5(x):
+    hi, lo = split(x)
+    return jnp.concatenate([hi, hi, lo, lo, hi], axis=1)
+
+
+def right5(x):
     hi, mid, lo = split3(x)
-    return jnp.concatenate([hi, hi, mid, hi, mid, lo], axis=1)
-
-
-def right6(x, axis):
-    hi, mid, lo = split3(x)
-    return jnp.concatenate([hi, mid, hi, lo, mid, hi], axis=axis)
+    return jnp.concatenate([hi, mid, hi, mid, lo], axis=0)
 
 
 def left4(x):
@@ -88,19 +88,24 @@
     return e, g + g1, l + l1
 
 
-def local_kernel(blocks, length, a_ref, m_ref, p_ref, q_ref, e_ref, l_ref, g_ref, tot_ref, acc_e, acc_l, acc_g):
+def local_kernel(blocks, length, a_ref, m_ref, p_ref, q_ref, e_ref, l_ref, g_ref, tot_ref, acc_e, acc_l, acc_g, at):
     s = pl.program_id(0)
     n = a_ref.shape[0]
     last_dev = jnp.logical_and(
         lax.axis_index("grp") == lax.axis_size("grp") - 1,
         lax.axis_index("ta") == lax.axis_size("ta") - 1,
     )
-    at = right6(a_ref[...], 1)
-    rows = [p_ref[b, 0] for b in range(blocks)] + [wide(m_ref[b, 0]) for b in range(blocks)]
-    moved = mm_t(left6(jnp.concatenate(rows, axis=0)), at)
+
+    @pl.when(s == 0)
+    def _():
+        at[...] = right5(a_ref[...].T)
+
+    spot = [pl.ds(b * length + length - 1 - s, 1) for b in range(blocks)]
+    rows = [p_ref[b, 0] for b in range(blocks)] + [wide(m_ref[spot[b]]) for b in range(blocks)]
+    moved = mm(left5(jnp.concatenate(rows, axis=0)), at[...])
     gains = []
     for b in range(blocks):
-        gain = mm(left6(moved[b * n:(b + 1) * n]), right6(q_ref[b, 0], 0))
+        gain = mm(left4(moved[b * n:(b + 1) * n]), right4(q_ref[b, 0], 0))
         if b == blocks - 1:
             gain = jnp.where(jnp.logical_and(last_dev, s == 0), jnp.zeros_like(gain), gain)
         gains.append(gain)
@@ -109,10 +114,10 @@
         start = blocks * n + b * PAD
         l, g = push(inner - moved[b * n:(b + 1) * n], row - moved[start:start + 1], right4(gains[b], 1), left4)
         l = l + p_ref[b, 0]
-        g = g + m_ref[b, 0]
+        g = g + m_ref[spot[b]]
         e_ref[b, 0] = e
         l_ref[b, 0] = l
-        g_ref[b, 0] = g
+        g_ref[spot[b]] = g
         acc_e[b] = e
         acc_l[b] = l
         acc_g[b] = jnp.broadcast_to(g, (8, n))
@@ -143,19 +148,26 @@
         tot_ref[half + n:2 * half] = jnp.zeros((PAD, n), F32)
 
 
-def exchange_kernel(sizes, t_ref, o_ref, tot, exc, got, s_sem, r_sem, s2_sem, r2_sem):
+def exchange_kernel(sizes, t_ref, o_ref, tot, exc, got, s_sem, r_sem, s2_sem, r2_sem, s3_sem):
     n = t_ref.shape[1]
     half = n + PAD
     grp, ta = lax.axis_index("grp"), lax.axis_index("ta")
     core = lax.rem(ta, 2)
     sib = (grp, ta + 1 - 2 * core)
     partners = []
+    relay = -1
     for name, size in sizes:
         step = 1
         while step < size:
             pos = ta if name == "ta" else grp
             bit = lax.rem(lax.div(pos, step), 2)
             other = pos + step - 2 * step * bit
+            if name == "ta" and step == 4:
+                below = lax.rem(lax.div(pos, 2), 2)
+                near = (grp, pos + 2 - 4 * below)
+                edge = below != bit
+                other = other + 2 - 4 * below
+                relay = len(partners)
             partners.append(((grp, other) if name == "ta" else (other, ta), bit))
             step *= 2
     rounds = len(partners)
@@ -181,32 +193,63 @@
     def pick(c, x, y):
         return tuple(jnp.where(c, i, j) for i, j in zip(x, y))
 
+    def extend(k):
+        was_low = partners[k - 1][1] == 0
+        if k == 1:
+            eye = (lax.broadcasted_iota(jnp.int32, (n, n), 0) == lax.broadcasted_iota(jnp.int32, (n, n), 1)).astype(F32)
+            write(exc.at[1], pick(was_low, read(got.at[0]), (eye, jnp.zeros((1, n), F32), jnp.zeros((n, n), F32))))
+        else:
+            mine = read(exc.at[(k - 1) % 2])
+            write(exc.at[k % 2], pick(was_low, compose(mine, read(got.at[k - 1])), mine))
+
+    def guard(k):
+        return pl.when(edge) if k == relay else (lambda f: f())
+
     for k, (dev, bit) in enumerate(partners):
         final = k == rounds - 1
         low = bit == 0
         src = t_ref if k == 0 else tot.at[k]
         if k == 0:
-            send = copy(src, got.at[k], s_sem.at[k], r_sem.at[k], dev)
+            send = copy(src, got.at[k], s_sem.at[k, 0], r_sem.at[k, 0], dev)
             send.start()
+            send.wait()
         else:
             size = half // 2 if final else half
-            rows = pl.ds(pl.multiple_of(core * size, 8), size)
-            send = copy(src.at[rows], got.at[k, rows], s_sem.at[k], r_sem.at[k], dev)
-            send.start()
-        if k > 1:
-            old, new = exc.at[(k - 1) % 2], got.at[k - 1]
-            was_low = partners[k - 1][1] == 0
-            mine = read(old)
-            write(exc.at[k % 2], pick(was_low, compose(mine, read(new)), mine))
-        elif k == 1:
-            was_low = partners[0][1] == 0
-            eye = (lax.broadcasted_iota(jnp.int32, (n, n), 0) == lax.broadcasted_iota(jnp.int32, (n, n), 1)).astype(F32)
-            write(exc.at[1], pick(was_low, read(got.at[0]), (eye, jnp.zeros((1, n), F32), jnp.zeros((n, n), F32))))
-        send.wait()
-        if k > 0:
-            swap = copy(got.at[k, rows], got.at[k, rows], s2_sem.at[k], r2_sem.at[k], sib)
-            swap.start()
-            swap.wait()
+            count = 2 if final else 4
+            each = size // count // 8 * 8
+            sends, swaps, passes = [], [], []
+            for c in range(count):
+                length = each if c < count - 1 else size - each * (count - 1)
+                rows = pl.ds(pl.multiple_of(core * size + c * each, 8), length)
+                spot = got.at[k, rows]
+                sends.append(copy(src.at[rows], spot, s_sem.at[k, c], r_sem.at[k, c], dev))
+                swaps.append(copy(spot, spot, s2_sem.at[k, c], r2_sem.at[k, c], sib))
+                if k == relay:
+                    passes.append(copy(spot, spot, s3_sem.at[c], r_sem.at[k, c], near))
+
+            @guard(k)
+            def _():
+                for send in sends:
+                    send.start()
+
+            if k != relay:
+                extend(k)
+            for c in range(count):
+                sends[c].wait_recv()
+                if k == relay:
+                    pl.when(edge)(passes[c].start)
+                swaps[c].start()
+                if k == relay and c == 1:
+                    extend(k)
+            for swap in swaps:
+                swap.wait()
+
+            @guard(k)
+            def _():
+                for send in sends:
+                    send.wait_send()
+                for send in passes:
+                    send.wait_send()
         if not final:
             mine, theirs = read(src), read(got.at[k])
             write(tot.at[k + 1], compose(pick(low, mine, theirs), pick(low, theirs, mine)))
@@ -218,7 +261,7 @@
     o_ref[n:half] = wide(jnp.where(low, g, mine[1]))
 
 
-def apply_kernel(length, c_ref, e_ref, l_ref, g_ref, m_ref, o_ref, carry):
+def apply_kernel(blocks, length, c_ref, e_ref, l_ref, g_ref, m_ref, o_ref, carry):
     n = e_ref.shape[-1]
 
     @pl.when(pl.program_id(0) == 0)
@@ -230,9 +273,10 @@
         e = e_ref[0, i]
         l, g = push(mm(left(e), cov), mean, right_t(e))
         l = l + l_ref[0, i]
-        g = g + g_ref[0, i]
+        spot = pl.ds((blocks - 1 - pl.program_id(0)) * length + i, 1)
+        g = g + g_ref[spot]
         o_ref[0, i] = l
-        m_ref[0, i] = g
+        m_ref[spot] = g
     carry[0:n] = l
     carry[n:n + PAD] = wide(g)
 
@@ -243,7 +287,6 @@
     length = steps // blocks
     half = n + PAD
     mat = (blocks, length, n, n)
-    vec = (blocks, length, 1, n)
     limit = 56 * 1024 * 1024
     flops = 2 * n * n * n * 3
     by_pos = lambda shape: pl.BlockSpec((blocks, 1) + shape, lambda s: (0, length - 1 - s, 0, 0))
@@ -251,22 +294,23 @@
     e, l, g, total = pl.pallas_call(
         functools.partial(local_kernel, blocks, length),
         grid=(length,),
-        in_specs=[whole((n, n)), by_pos((1, n)), by_pos((n, n)), by_pos((n, n))],
-        out_specs=[by_pos((n, n)), by_pos((n, n)), by_pos((1, n)), whole((2 * half, n))],
+        in_specs=[whole((n, n)), whole((steps, n)), by_pos((n, n)), by_pos((n, n))],
+        out_specs=[by_pos((n, n)), by_pos((n, n)), whole((steps, n)), whole((2 * half, n))],
         out_shape=[
             jax.ShapeDtypeStruct(mat, F32),
             jax.ShapeDtypeStruct(mat, F32),
-            jax.ShapeDtypeStruct(vec, F32),
+            jax.ShapeDtypeStruct((steps, n), F32),
             jax.ShapeDtypeStruct((2 * half, n), F32),
         ],
         scratch_shapes=[
             pltpu.VMEM((blocks, n, n), F32),
             pltpu.VMEM((blocks, n, n), F32),
             pltpu.VMEM((blocks, 8, n), F32),
+            pltpu.VMEM((5 * n, n), BF16),
         ],
         compiler_params=pltpu.CompilerParams(vmem_limit_bytes=limit),
         cost_estimate=pl.CostEstimate(flops=80 * flops, bytes_accessed=16 * steps * n * n, transcendentals=0),
-    )(transition, filtered_mean.reshape(vec), filtered_cov.reshape(mat), pred_precision.reshape(mat))
+    )(transition, filtered_mean, filtered_cov.reshape(mat), pred_precision.reshape(mat))
 
     sizes = (("ta", lax.axis_size("ta")), ("grp", lax.axis_size("grp")))
     rounds = sum(size.bit_length() - 1 for _, size in sizes)
@@ -280,22 +324,22 @@
             pltpu.VMEM((rounds, 2 * half, n), F32),
             pltpu.VMEM((2, 2 * half, n), F32),
             pltpu.VMEM((rounds, 2 * half, n), F32),
-        ] + [pltpu.SemaphoreType.DMA((rounds,))] * 4,
+        ] + [pltpu.SemaphoreType.DMA((rounds, 4))] * 4 + [pltpu.SemaphoreType.DMA((4,))],
         compiler_params=pltpu.CompilerParams(
             vmem_limit_bytes=limit, collective_id=0, has_side_effects=True),
     )(total)
 
     back = lambda shape: pl.BlockSpec((1, length) + shape, lambda s: (blocks - 1 - s, 0, 0, 0))
     mean, cov = pl.pallas_call(
-        functools.partial(apply_kernel, length),
+        functools.partial(apply_kernel, blocks, length),
         grid=(blocks,),
-        in_specs=[whole((half, n)), back((n, n)), back((n, n)), back((1, n))],
-        out_specs=[back((1, n)), back((n, n))],
-        out_shape=[jax.ShapeDtypeStruct(vec, F32), jax.ShapeDtypeStruct(mat, F32)],
+        in_specs=[whole((half, n)), back((n, n)), back((n, n)), whole((steps, n))],
+        out_specs=[whole((steps, n)), back((n, n))],
+        out_shape=[jax.ShapeDtypeStruct((steps, n), F32), jax.ShapeDtypeStruct(mat, F32)],
         scratch_shapes=[pltpu.VMEM((half, n), F32)],
         compiler_params=pltpu.CompilerParams(vmem_limit_bytes=limit),
     )(carried, e, l, g)
-    return mean.reshape(steps, n), cov.reshape(steps, n, n)
+    return mean, cov.reshape(steps, n, n)
 
 
 def solution(mesh):

time: 91.3 us -> 81.2 us (0.89)
  Pallas kernels: 87.6 us -> 80.3 us
  local copies, waits for them, and re-layouts: 1.96 us -> 0 us
    pallas_call x1, Pallas kernels: 26.7 us -> 22.9 us  [body(): pl.pallas_call(functools.partial(local_kernel, blocks, length), grid=(len...]
    pallas_call x1, Pallas kernels: 52.2 us -> 49 us  [body(): pl.pallas_call(functools.partial(exchange_kernel, sizes), in_specs=[vmem]...]
    reshape x2 -> x0, local copies, waits for them, and re-layouts: 1.96 us -> none  [the longest x1 1.34 us: body(): filtered_mean.reshape(vec)]
where the time goes in v2:
time: 81.2 us; the launch traced here: 81 us
  Pallas kernels  80.3 us (99%)
    pallas_call x1, Pallas kernels, body(): pl.pallas_call(functools.partial(exchange_kernel, sizes), in_specs=[vmem]...  49 us
    pallas_call x1, Pallas kernels, body(): pl.pallas_call(functools.partial(local_kernel, blocks, length), grid=(len...  22.9 us
    pallas_call x1, Pallas kernels, body(): pl.pallas_call(functools.partial(apply_kernel, blocks, length), grid=(blo...  8.44 us

profile of v2, /device:TPU:0, one launch (start us, length us, event | category | flops | bytes accessed | tf_op | source)
XLA Modules:
  0.0 81.0 jit_solution(10686575554151012854)
XLA Ops:
  0.6 22.9 %shard_map.59 = (f32[4,4,256,256]{3,2,1,0:T(8,128)}, f32[4,4,256,256]{3,2,1,0:T(8,128)}, f32[16,256]{1,0:T(8,128)}, f32[544,256]{1,0:T(8,128)}) custom-call(f32[256,256]{1,0:T(8,128)} %a_ref.1, f32[16,256]{1,0:T(8,128)} %m_ref.1, f32[4,4,256,256]{3,2,1,0:T(8,128)} %bitcast.3, f32[4,4,256,256]{3,2,1,0:T(8,128)} %bitcast.4), custom_call_target="tpu_custom_call" | custom-call | flops 8053063680 | bytes 16777216 | tf_op jit(solution)/shard_map/pallas_call | solution.py:294
  23.6 49.0 %shard_map.60.c_ref = f32[272,256]{1,0:T(8,128)} custom-call(f32[544,256]{1,0:T(8,128)} %get-tuple-element.8.t_ref), custom_call_target="tpu_custom_call" | custom-call | tf_op jit(solution)/shard_map/pallas_call | solution.py:318
  72.5 8.4 %shard_map.61 = (f32[16,256]{1,0:T(8,128)}, f32[4,4,256,256]{3,2,1,0:T(8,128)}) custom-call(f32[272,256]{1,0:T(8,128)} %shard_map.60.c_ref, f32[4,4,256,256]{3,2,1,0:T(8,128)} %get-tuple-element.9.e_ref, f32[4,4,256,256]{3,2,1,0:T(8,128)} %get-tuple-element.10.l_ref, f32[16,256]{1,0:T(8,128)} %get-tuple-element.11.g_ref), custom_call_target="tpu_custom_call" | custom-call | tf_op jit(solution)/shard_map/pallas_call | solution.py:333

commit v3 on v2

--- a/solution.py
+++ b/solution.py
@@ -33,31 +33,8 @@
     return jnp.concatenate([hi, lo, hi], axis=1)
 
 
-def split3(x):
-    hi = x.astype(BF16)
-    rest = x - hi.astype(F32)
-    mid = rest.astype(BF16)
-    return hi, mid, (rest - mid.astype(F32)).astype(BF16)
-
-
-def left5(x):
-    hi, lo = split(x)
-    return jnp.concatenate([hi, hi, lo, lo, hi], axis=1)
-
-
-def right5(x):
-    hi, mid, lo = split3(x)
-    return jnp.concatenate([hi, mid, hi, mid, lo], axis=0)
-
-
-def left4(x):
-    hi, lo = split(x)
-    return jnp.concatenate([hi, hi, lo, lo], axis=1)
-
-
-def right4(x, axis):
-    hi, lo = split(x)
-    return jnp.concatenate([hi, lo, hi, lo], axis=axis)
+def unit(n):
+    return (lax.broadcasted_iota(jnp.int32, (n, n), 0) == lax.broadcasted_iota(jnp.int32, (n, n), 1)).astype(F32)
 
 
 def mm(a3, b3):
@@ -72,9 +49,12 @@
     return jnp.broadcast_to(row[:1, :], (PAD, row.shape[1]))
 
 
-def push(inner, row, e_t, cut=left):
+def push(inner, row, e_t, near=False):
     n = inner.shape[0]
-    out = mm_t(cut(jnp.concatenate([inner, wide(row)], axis=0)), e_t)
+    both = jnp.concatenate([inner, wide(row)], axis=0)
+    out = mm_t(left(both), e_t)
+    if near:
+        out = both + out
     return out[:n], out[n:n + 1]
 
 
@@ -98,21 +78,23 @@
 
     @pl.when(s == 0)
     def _():
-        at[...] = right5(a_ref[...].T)
+        at[...] = right((a_ref[...] - unit(n)).T)
 
     spot = [pl.ds(b * length + length - 1 - s, 1) for b in range(blocks)]
     rows = [p_ref[b, 0] for b in range(blocks)] + [wide(m_ref[spot[b]]) for b in range(blocks)]
-    moved = mm(left5(jnp.concatenate(rows, axis=0)), at[...])
+    rows = jnp.concatenate(rows, axis=0)
+    moved = rows + mm(left(rows), at[...])
     gains = []
+    eye = unit(n)
     for b in range(blocks):
-        gain = mm(left4(moved[b * n:(b + 1) * n]), right4(q_ref[b, 0], 0))
+        gain = mm(left(moved[b * n:(b + 1) * n]), right(q_ref[b, 0]))
         if b == blocks - 1:
             gain = jnp.where(jnp.logical_and(last_dev, s == 0), jnp.zeros_like(gain), gain)
         gains.append(gain)
 
     def finish(b, e, inner, row):
         start = blocks * n + b * PAD
-        l, g = push(inner - moved[b * n:(b + 1) * n], row - moved[start:start + 1], right4(gains[b], 1), left4)
+        l, g = push(inner - moved[b * n:(b + 1) * n], row - moved[start:start + 1], right_t(gains[b] - eye), True)
         l = l + p_ref[b, 0]
         g = g + m_ref[spot[b]]
         e_ref[b, 0] = e
@@ -130,9 +112,9 @@
     @pl.when(s > 0)
     def _():
         for b in range(blocks):
-            gl = left4(gains[b])
-            e = mm(gl, right4(acc_e[b], 0))
-            inner = mm(gl, right4(acc_l[b], 0))
+            gl = left(gains[b] - eye)
+            e = acc_e[b] + mm(gl, right(acc_e[b]))
+            inner = acc_l[b] + mm(gl, right(acc_l[b]))
             finish(b, e, inner, acc_g[b][:1])
 
     @pl.when(s == length - 1)
@@ -196,7 +178,7 @@
     def extend(k):
         was_low = partners[k - 1][1] == 0
         if k == 1:
-            eye = (lax.broadcasted_iota(jnp.int32, (n, n), 0) == lax.broadcasted_iota(jnp.int32, (n, n), 1)).astype(F32)
+            eye = unit(n)
             write(exc.at[1], pick(was_low, read(got.at[0]), (eye, jnp.zeros((1, n), F32), jnp.zeros((n, n), F32))))
         else:
             mine = read(exc.at[(k - 1) % 2])
@@ -306,7 +288,7 @@
             pltpu.VMEM((blocks, n, n), F32),
             pltpu.VMEM((blocks, n, n), F32),
             pltpu.VMEM((blocks, 8, n), F32),
-            pltpu.VMEM((5 * n, n), BF16),
+            pltpu.VMEM((3 * n, n), BF16),
         ],
         compiler_params=pltpu.CompilerParams(vmem_limit_bytes=limit),
         cost_estimate=pl.CostEstimate(flops=80 * flops, bytes_accessed=16 * steps * n * n, transcendentals=0),

time: 81.2 us -> 76.8 us (0.946)
  Pallas kernels: 80.3 us -> 75.9 us
    pallas_call x1, Pallas kernels: 22.9 us -> 18.5 us  [body(): pl.pallas_call(functools.partial(local_kernel, blocks, length), grid=(len...]
where the time goes in v3:
time: 76.8 us; the launch traced here: 76.6 us
  Pallas kernels  75.9 us (99%)
    pallas_call x1, Pallas kernels, body(): pl.pallas_call(functools.partial(exchange_kernel, sizes), in_specs=[vmem]...  49 us
    pallas_call x1, Pallas kernels, body(): pl.pallas_call(functools.partial(local_kernel, blocks, length), grid=(len...  18.5 us
    pallas_call x1, Pallas kernels, body(): pl.pallas_call(functools.partial(apply_kernel, blocks, length), grid=(blo...  8.44 us

profile of v3, /device:TPU:0, one launch (start us, length us, event | category | flops | bytes accessed | tf_op | source)
XLA Modules:
  0.0 76.6 jit_solution(4218454849716009468)
XLA Ops:
  0.6 18.5 %shard_map.59 = (f32[4,4,256,256]{3,2,1,0:T(8,128)}, f32[4,4,256,256]{3,2,1,0:T(8,128)}, f32[16,256]{1,0:T(8,128)}, f32[544,256]{1,0:T(8,128)}) custom-call(f32[256,256]{1,0:T(8,128)} %a_ref.1, f32[16,256]{1,0:T(8,128)} %m_ref.1, f32[4,4,256,256]{3,2,1,0:T(8,128)} %bitcast.3, f32[4,4,256,256]{3,2,1,0:T(8,128)} %bitcast.4), custom_call_target="tpu_custom_call" | custom-call | flops 8053063680 | bytes 16777216 | tf_op jit(solution)/shard_map/pallas_call | solution.py:276
  19.1 49.0 %shard_map.60.c_ref = f32[272,256]{1,0:T(8,128)} custom-call(f32[544,256]{1,0:T(8,128)} %get-tuple-element.8.t_ref), custom_call_target="tpu_custom_call" | custom-call | tf_op jit(solution)/shard_map/pallas_call | solution.py:300
  68.1 8.4 %shard_map.61 = (f32[16,256]{1,0:T(8,128)}, f32[4,4,256,256]{3,2,1,0:T(8,128)}) custom-call(f32[272,256]{1,0:T(8,128)} %shard_map.60.c_ref, f32[4,4,256,256]{3,2,1,0:T(8,128)} %get-tuple-element.9.e_ref, f32[4,4,256,256]{3,2,1,0:T(8,128)} %get-tuple-element.10.l_ref, f32[16,256]{1,0:T(8,128)} %get-tuple-element.11.g_ref), custom_call_target="tpu_custom_call" | custom-call | tf_op jit(solution)/shard_map/pallas_call | solution.py:315

commit v4 on v3

--- a/solution.py
+++ b/solution.py
@@ -66,6 +66,30 @@
     e = mm(e1l, right(e2)) if want_e else None
     l, g = push(inner, g2, right_t(e1))
     return e, g + g1, l + l1
+
+
+def layout(n):
+    tri = n // 2 + n // 4
+    return tri, tri + PAD, tri + PAD + n
+
+
+def load(ref, want_e=True):
+    n = ref.shape[-1]
+    h, (tri, start, full) = n // 2, layout(n)
+    top, low = ref[0:h], ref[h:tri]
+    low = jnp.concatenate([low[:, :h], low[:, h:]], axis=0)
+    low = jnp.concatenate([top[:, h:].T, low], axis=1)
+    return ref[start:full] if want_e else None, ref[tri:tri + 8][:1], jnp.concatenate([top, low], axis=0)
+
+
+def store(ref, val):
+    e, g, l = val
+    n = ref.shape[-1]
+    h, q, (tri, start, full) = n // 2, n // 4, layout(n)
+    ref[0:h] = l[:h]
+    ref[h:tri] = jnp.concatenate([l[h:h + q, h:], l[h + q:, h:]], axis=1)
+    ref[tri:start] = wide(g)
+    ref[start:full] = e
 
 
 def local_kernel(blocks, length, a_ref, m_ref, p_ref, q_ref, e_ref, l_ref, g_ref, tot_ref, acc_e, acc_l, acc_g, at):
@@ -122,17 +146,12 @@
         parts = [(acc_e[b], acc_g[b][:1], acc_l[b]) for b in range(blocks)]
         while len(parts) > 1:
             parts = [compose(parts[i], parts[i + 1]) for i in range(0, len(parts), 2)]
-        e, g, l = parts[0]
-        half = n + PAD
-        tot_ref[0:n] = l
-        tot_ref[n:half] = wide(g)
-        tot_ref[half:half + n] = e
-        tot_ref[half + n:2 * half] = jnp.zeros((PAD, n), F32)
+        store(tot_ref, parts[0])
 
 
 def exchange_kernel(sizes, t_ref, o_ref, tot, exc, got, s_sem, r_sem, s2_sem, r2_sem, s3_sem):
     n = t_ref.shape[1]
-    half = n + PAD
+    tri, start, full = layout(n)
     grp, ta = lax.axis_index("grp"), lax.axis_index("ta")
     core = lax.rem(ta, 2)
     sib = (grp, ta + 1 - 2 * core)
@@ -162,16 +181,6 @@
         return pltpu.make_async_remote_copy(
             src_ref=src, dst_ref=dst, send_sem=a, recv_sem=b, device_id=dev, device_id_type=MESH)
 
-    def read(ref):
-        return ref[half:half + n], ref[n:n + 8][:1], ref[0:n]
-
-    def write(ref, val):
-        e, g, l = val
-        ref[0:n] = l
-        ref[n:half] = wide(g)
-        ref[half:half + n] = e
-        ref[half + n:2 * half] = jnp.zeros((PAD, n), F32)
-
     def pick(c, x, y):
         return tuple(jnp.where(c, i, j) for i, j in zip(x, y))
 
@@ -179,10 +188,10 @@
         was_low = partners[k - 1][1] == 0
         if k == 1:
             eye = unit(n)
-            write(exc.at[1], pick(was_low, read(got.at[0]), (eye, jnp.zeros((1, n), F32), jnp.zeros((n, n), F32))))
+            store(exc.at[1], pick(was_low, load(got.at[0]), (eye, jnp.zeros((1, n), F32), jnp.zeros((n, n), F32))))
         else:
-            mine = read(exc.at[(k - 1) % 2])
-            write(exc.at[k % 2], pick(was_low, compose(mine, read(got.at[k - 1])), mine))
+            mine = load(exc.at[(k - 1) % 2])
+            store(exc.at[k % 2], pick(was_low, compose(mine, load(got.at[k - 1])), mine))
 
     def guard(k):
         return pl.when(edge) if k == relay else (lambda f: f())
@@ -196,7 +205,7 @@
             send.start()
             send.wait()
         else:
-            size = half // 2 if final else half
+            size = (start if final else full) // 2
             count = 2 if final else 4
             each = size // count // 8 * 8
             sends, swaps, passes = [], [], []
@@ -233,14 +242,12 @@
                 for send in passes:
                     send.wait_send()
         if not final:
-            mine, theirs = read(src), read(got.at[k])
-            write(tot.at[k + 1], compose(pick(low, mine, theirs), pick(low, theirs, mine)))
-    mine = read(exc.at[(rounds - 1) % 2])
-    ref = got.at[rounds - 1]
-    later = (None, ref[n:n + 8][:1], ref[0:n])
-    _, g, l = compose(mine, later, want_e=False)
+            mine, theirs = load(src), load(got.at[k])
+            store(tot.at[k + 1], compose(pick(low, mine, theirs), pick(low, theirs, mine)))
+    mine = load(exc.at[(rounds - 1) % 2])
+    _, g, l = compose(mine, load(got.at[rounds - 1], False), want_e=False)
     o_ref[0:n] = jnp.where(low, l, mine[2])
-    o_ref[n:half] = wide(jnp.where(low, g, mine[1]))
+    o_ref[n:n + PAD] = wide(jnp.where(low, g, mine[1]))
 
 
 def apply_kernel(blocks, length, c_ref, e_ref, l_ref, g_ref, m_ref, o_ref, carry):
@@ -277,12 +284,12 @@
         functools.partial(local_kernel, blocks, length),
         grid=(length,),
         in_specs=[whole((n, n)), whole((steps, n)), by_pos((n, n)), by_pos((n, n))],
-        out_specs=[by_pos((n, n)), by_pos((n, n)), whole((steps, n)), whole((2 * half, n))],
+        out_specs=[by_pos((n, n)), by_pos((n, n)), whole((steps, n)), whole((layout(n)[2], n))],
         out_shape=[
             jax.ShapeDtypeStruct(mat, F32),
             jax.ShapeDtypeStruct(mat, F32),
             jax.ShapeDtypeStruct((steps, n), F32),
-            jax.ShapeDtypeStruct((2 * half, n), F32),
+            jax.ShapeDtypeStruct((layout(n)[2], n), F32),
         ],
         scratch_shapes=[
             pltpu.VMEM((blocks, n, n), F32),
@@ -303,9 +310,9 @@
         out_specs=vmem,
         out_shape=jax.ShapeDtypeStruct((half, n), F32),
         scratch_shapes=[
-            pltpu.VMEM((rounds, 2 * half, n), F32),
-            pltpu.VMEM((2, 2 * half, n), F32),
-            pltpu.VMEM((rounds, 2 * half, n), F32),
+            pltpu.VMEM((rounds, layout(n)[2], n), F32),
+            pltpu.VMEM((2, layout(n)[2], n), F32),
+            pltpu.VMEM((rounds, layout(n)[2], n), F32),
         ] + [pltpu.SemaphoreType.DMA((rounds, 4))] * 4 + [pltpu.SemaphoreType.DMA((4,))],
         compiler_params=pltpu.CompilerParams(
             vmem_limit_bytes=limit, collective_id=0, has_side_effects=True),

time: 76.8 us -> 73.4 us (0.956)
  Pallas kernels: 75.9 us -> 72.6 us
    pallas_call x1, Pallas kernels: 49 us -> 45.7 us  [body(): pl.pallas_call(functools.partial(exchange_kernel, sizes), in_specs=[vmem]...]
where the time goes in v4:
time: 73.4 us; the launch traced here: 73.2 us
  Pallas kernels  72.6 us (99%)
    pallas_call x1, Pallas kernels, body(): pl.pallas_call(functools.partial(exchange_kernel, sizes), in_specs=[vmem]...  45.7 us
    pallas_call x1, Pallas kernels, body(): pl.pallas_call(functools.partial(local_kernel, blocks, length), grid=(len...  18.5 us
    pallas_call x1, Pallas kernels, body(): pl.pallas_call(functools.partial(apply_kernel, blocks, length), grid=(blo...  8.44 us

profile of v4, /device:TPU:0, one launch (start us, length us, event | category | flops | bytes accessed | tf_op | source)
XLA Modules:
  0.0 73.2 jit_solution(8409378151617149710)
XLA Ops:
  0.6 18.5 %shard_map.59 = (f32[4,4,256,256]{3,2,1,0:T(8,128)}, f32[4,4,256,256]{3,2,1,0:T(8,128)}, f32[16,256]{1,0:T(8,128)}, f32[464,256]{1,0:T(8,128)}) custom-call(f32[256,256]{1,0:T(8,128)} %a_ref.1, f32[16,256]{1,0:T(8,128)} %m_ref.1, f32[4,4,256,256]{3,2,1,0:T(8,128)} %bitcast.3, f32[4,4,256,256]{3,2,1,0:T(8,128)} %bitcast.4), custom_call_target="tpu_custom_call" | custom-call | flops 8053063680 | bytes 16777216 | tf_op jit(solution)/shard_map/pallas_call | solution.py:283
  19.1 45.7 %shard_map.60.c_ref = f32[272,256]{1,0:T(8,128)} custom-call(f32[464,256]{1,0:T(8,128)} %get-tuple-element.8.t_ref), custom_call_target="tpu_custom_call" | custom-call | tf_op jit(solution)/shard_map/pallas_call | solution.py:307
  64.8 8.4 %shard_map.61 = (f32[16,256]{1,0:T(8,128)}, f32[4,4,256,256]{3,2,1,0:T(8,128)}) custom-call(f32[272,256]{1,0:T(8,128)} %shard_map.60.c_ref, f32[4,4,256,256]{3,2,1,0:T(8,128)} %get-tuple-element.9.e_ref, f32[4,4,256,256]{3,2,1,0:T(8,128)} %get-tuple-element.10.l_ref, f32[16,256]{1,0:T(8,128)} %get-tuple-element.11.g_ref), custom_call_target="tpu_custom_call" | custom-call | tf_op jit(solution)/shard_map/pallas_call | solution.py:322

commit v5 on v4

--- a/solution.py
+++ b/solution.py
@@ -258,9 +258,10 @@
         carry[...] = c_ref[...]
 
     cov, mean = right(carry[0:n]), carry[n:n + 8][:1]
+    inner = mm(left(jnp.concatenate([e_ref[0, i] for i in range(length)], axis=0)), cov)
     for i in reversed(range(length)):
         e = e_ref[0, i]
-        l, g = push(mm(left(e), cov), mean, right_t(e))
+        l, g = push(inner[i * n:(i + 1) * n], mean, right_t(e))
         l = l + l_ref[0, i]
         spot = pl.ds((blocks - 1 - pl.program_id(0)) * length + i, 1)
         g = g + g_ref[spot]

time: 73.4 us -> 75.1 us (1.023)
  Pallas kernels: 72.6 us -> 74.2 us
    pallas_call x1, Pallas kernels: 8.44 us -> 10.1 us  [body(): pl.pallas_call(functools.partial(apply_kernel, blocks, length), grid=(blo...]
where the time goes in v5:
time: 75.1 us; the launch traced here: 74.8 us
  Pallas kernels  74.2 us (99%)
    pallas_call x1, Pallas kernels, body(): pl.pallas_call(functools.partial(exchange_kernel, sizes), in_specs=[vmem]...  45.7 us
    pallas_call x1, Pallas kernels, body(): pl.pallas_call(functools.partial(local_kernel, blocks, length), grid=(len...  18.5 us
    pallas_call x1, Pallas kernels, body(): pl.pallas_call(functools.partial(apply_kernel, blocks, length), grid=(blo...  10.1 us

profile of v5, /device:TPU:0, one launch (start us, length us, event | category | flops | bytes accessed | tf_op | source)
XLA Modules:
  0.0 74.8 jit_solution(5395969141120358859)
XLA Ops:
  0.6 18.5 %shard_map.59 = (f32[4,4,256,256]{3,2,1,0:T(8,128)}, f32[4,4,256,256]{3,2,1,0:T(8,128)}, f32[16,256]{1,0:T(8,128)}, f32[464,256]{1,0:T(8,128)}) custom-call(f32[256,256]{1,0:T(8,128)} %a_ref.1, f32[16,256]{1,0:T(8,128)} %m_ref.1, f32[4,4,256,256]{3,2,1,0:T(8,128)} %bitcast.3, f32[4,4,256,256]{3,2,1,0:T(8,128)} %bitcast.4), custom_call_target="tpu_custom_call" | custom-call | flops 8053063680 | bytes 16777216 | tf_op jit(solution)/shard_map/pallas_call | solution.py:284
  19.1 45.7 %shard_map.60.c_ref = f32[272,256]{1,0:T(8,128)} custom-call(f32[464,256]{1,0:T(8,128)} %get-tuple-element.8.t_ref), custom_call_target="tpu_custom_call" | custom-call | tf_op jit(solution)/shard_map/pallas_call | solution.py:308
  64.8 10.1 %shard_map.61 = (f32[16,256]{1,0:T(8,128)}, f32[4,4,256,256]{3,2,1,0:T(8,128)}) custom-call(f32[272,256]{1,0:T(8,128)} %shard_map.60.c_ref, f32[4,4,256,256]{3,2,1,0:T(8,128)} %get-tuple-element.9.e_ref, f32[4,4,256,256]{3,2,1,0:T(8,128)} %get-tuple-element.10.l_ref, f32[16,256]{1,0:T(8,128)} %get-tuple-element.11.g_ref), custom_call_target="tpu_custom_call" | custom-call | tf_op jit(solution)/shard_map/pallas_call | solution.py:323
